TPU v7x, 32 devices: a whole 2x2x4 slice. The times are simulated.
32 devices in a mesh: grp: 4 (over z), seq: 8 (over y, x, core).
Axes of the slice: x: 2, y: 2, z: 4, core: 2. Of those that a mesh axis runs over, the one named last changes fastest.
Arguments:
- queries: bfloat16 [4096, 6144], P(('grp', 'seq')), may hold values from -64 to 64
- keys_values: bfloat16 [4096, 768], P(('grp', 'seq')), may hold values from -6 to 6
- selection: int32 [64, 32], P(('grp', 'seq')), may hold values from -1 to 63, as said below
- gate_logits: bfloat16 [3, 4096, 32], P(None, ('grp', 'seq')), may hold values from -6 to 6
- pos_weight: bfloat16 [64, 384], replicated, may hold values from -0.75 to 0.75
- compress_weight: bfloat16 [384, 384], replicated, may hold values from -0.3125 to 0.3125
Outputs:
- attended: bfloat16 [4096, 6144], P(('grp', 'seq'))
Inputs may be any that keep to these rules, and one draw needn't show every extreme that they name: `selection`: A run is the 2 rows of one device; a segment is 16 consecutive rows. Row r lists, for each group, 16 distinct block numbers no greater than r, or -1 for unused entries. Within one group, the rows of a run list from each earlier segment exactly one block, and it lies in the run at the same place of that segment; from any other run of their own segment they list at most one block.
All inputs are finite; a program needn't handle non-finite values.
Results may differ from a plain program's by a relative error of at most 0.0055.
Values may be sent and summed in bfloat16 or wider, within the bound.
A program may use at most 128 MiB of HBM per device.

v0:
```python
import math
import jax
import jax.numpy as jnp
from jax import lax
from jax.sharding import PartitionSpec as P

HEAD_DIM = 192
GROUPS = 2
GROUP_HEADS = 16
HEADS = 32
BLOCK = 64
TOP = 16
CAP = 2
WINDOW = 128
NEG_FILL = -1e30


def from_behind(block, axis, distance):
    devices = range(lax.axis_size(axis))
    route = [(i - distance, i) for i in devices if i - distance in devices]
    return lax.ppermute(block, axis, route)


def attend(query_block, key_block, allowed, with_sink):
    head_dim = query_block.shape[-1]
    score_scale = head_dim ** (-0.5)
    scores = (
        jnp.einsum(
            "btghd,bgnd->bghtn",
            query_block,
            key_block[..., :head_dim],
            preferred_element_type=jnp.float32,
        )
        * score_scale
    )
    allowed_wide = allowed[:, :, None]
    scores = jnp.where(allowed_wide, scores, NEG_FILL)
    top_score = jnp.max(scores, axis=-1, keepdims=True)
    if with_sink:
        top_score = jnp.maximum(top_score, 0.0)
    weights = jnp.where(allowed_wide, jnp.exp(scores - top_score), 0.0)
    denominator = jnp.sum(weights, axis=-1, keepdims=True)
    if with_sink:
        denominator = denominator + jnp.exp(-top_score)
    rounded = weights.astype(jnp.bfloat16)
    blended = (
        jnp.einsum(
            "bghtn,bgnd->bghtd",
            rounded,
            key_block[..., head_dim:],
            preferred_element_type=jnp.float32,
        )
        / denominator
    )
    return jnp.transpose(blended, (0, 3, 1, 2, 4))


def by_heads(query_block, key_block, allowed, with_sink):
    head_count = query_block.shape[3]
    slab_width = math.gcd(4, head_count)

    def head_slab(slab_index):
        query_slab = lax.dynamic_slice_in_dim(query_block, slab_index * slab_width, slab_width, 3)
        return attend(query_slab, key_block, allowed, with_sink)

    stacked = lax.map(head_slab, jnp.arange(head_count // slab_width, dtype=jnp.int32))
    stacked = jnp.moveaxis(stacked, 0, 3)
    return stacked.reshape(stacked.shape[:3] + (head_count, stacked.shape[-1]))


def compress_blocks(keys_values, pos_weight, compress_weight):
    block_count = keys_values.shape[0] // BLOCK
    grouped = keys_values.reshape(block_count, BLOCK, GROUPS, 2 * HEAD_DIM).astype(jnp.float32)
    pooled = jnp.sum(grouped * pos_weight.astype(jnp.float32)[None, :, None, :], axis=1).astype(
        jnp.bfloat16
    )
    mapped = jnp.dot(
        pooled.reshape(block_count * GROUPS, 2 * HEAD_DIM),
        compress_weight,
        preferred_element_type=jnp.float32,
    )
    return mapped.astype(jnp.bfloat16).reshape(block_count, GROUPS, 2 * HEAD_DIM)


def plan_requests(unit_of, key_of, wanted, unit_count, key_count):
    hits = (
        wanted[:, None, None]
        & (unit_of[:, None, None] == jnp.arange(unit_count, dtype=jnp.int32)[None, :, None])
        & (key_of[:, None, None] == jnp.arange(key_count, dtype=jnp.int32)[None, None, :])
    )
    present = jnp.any(hits, axis=0)
    ordinal = jnp.cumsum(present.astype(jnp.int32), axis=1) - 1
    slot_of = jnp.sum(jnp.where(hits, ordinal[None], 0), axis=(1, 2))
    matches = present[:, :, None] & (
        ordinal[:, :, None] == jnp.arange(CAP, dtype=jnp.int32)[None, None, :]
    )
    requests = (
        jnp.sum(
            jnp.where(matches, jnp.arange(key_count, dtype=jnp.int32)[None, :, None] + 1, 0), axis=1
        )
        - 1
    )
    return (slot_of, requests)


def shards(queries, keys_values, selection, gate_logits, pos_weight, compress_weight):
    grp_index = lax.axis_index("grp")
    seq_index = lax.axis_index("seq")
    grp_count = lax.axis_size("grp")
    seq_count = lax.axis_size("seq")
    tok_count = queries.shape[0]
    dev_blocks = tok_count // BLOCK
    seg_tokens = tok_count * seq_count
    seg_blocks = seg_tokens // BLOCK
    all_blocks = seg_blocks * grp_count
    key_count = GROUPS * dev_blocks
    first_pos = (grp_index * seq_count + seq_index) * tok_count
    positions = first_pos + jnp.arange(tok_count, dtype=jnp.int32)
    local_view = keys_values.reshape(dev_blocks, BLOCK, GROUPS, 2 * HEAD_DIM)
    local_summary = jnp.transpose(
        compress_blocks(keys_values, pos_weight, compress_weight), (1, 0, 2)
    )
    summaries = lax.all_gather(local_summary, ("grp", "seq"), axis=1, tiled=True)
    picked = selection.reshape(dev_blocks, GROUPS, TOP)
    group_ids = jnp.broadcast_to(jnp.arange(GROUPS, dtype=jnp.int32)[None, :, None], picked.shape)
    flat_groups = group_ids.reshape(-1)
    flat_picks = picked.reshape(-1)
    clipped_flat = jnp.maximum(flat_picks, 0)
    segment_of = clipped_flat // seg_blocks
    key_of = flat_groups * dev_blocks + clipped_flat % dev_blocks
    wanted = (flat_picks >= 0) & (segment_of != grp_index)
    slot_of, requests = plan_requests(segment_of, key_of, wanted, grp_count, key_count)
    asked_clipped = jnp.maximum(
        lax.all_to_all(requests, "grp", split_axis=0, concat_axis=0, tiled=True), 0
    )
    received = lax.all_to_all(
        local_view[asked_clipped % dev_blocks, :, asked_clipped // dev_blocks, :],
        "grp",
        split_axis=0,
        concat_axis=0,
        tiled=True,
    )
    picks_clipped = jnp.maximum(picked, 0)
    pick_segment = picks_clipped // seg_blocks
    from_remote = received[pick_segment, slot_of.reshape(picked.shape)]
    segment = lax.all_gather(keys_values, "seq", axis=0, tiled=True)
    earlier_tail = from_behind(segment[seg_tokens - WINDOW :], "grp", 1)
    segment_view = segment.reshape(seg_blocks, BLOCK, GROUPS, 2 * HEAD_DIM)
    from_segment = segment_view[picks_clipped % seg_blocks, :, group_ids, :]
    start_row = jnp.maximum(seq_index * tok_count - WINDOW, 0)
    inside = lax.dynamic_slice_in_dim(segment, start_row, WINDOW, 0)
    before = jnp.where(seq_index == 0, earlier_tail, inside)
    own_rows = (pick_segment == grp_index)[..., None, None]
    chosen = jnp.where(own_rows, from_segment, from_remote).reshape(
        dev_blocks, GROUPS, TOP * BLOCK, 2 * HEAD_DIM
    )
    key_positions = (picks_clipped[..., None] * BLOCK + jnp.arange(BLOCK, dtype=jnp.int32)).reshape(
        dev_blocks, GROUPS, TOP * BLOCK
    )
    live_keys = jnp.repeat(picked >= 0, BLOCK, axis=2)
    block_positions = positions.reshape(dev_blocks, BLOCK)
    allowed_sel = live_keys[:, :, None, :] & (
        key_positions[:, :, None, :] <= block_positions[:, None, :, None]
    )
    query_blocks = queries.reshape(dev_blocks, BLOCK, GROUPS, GROUP_HEADS, HEAD_DIM)
    selected_branch = by_heads(query_blocks, chosen, allowed_sel, False).reshape(
        tok_count, GROUPS, GROUP_HEADS, HEAD_DIM
    )
    query_whole = queries.reshape(1, tok_count, GROUPS, GROUP_HEADS, HEAD_DIM)
    block_ends = jnp.arange(all_blocks, dtype=jnp.int32) * BLOCK + BLOCK - 1
    allowed_comp = (block_ends[None, :] <= positions[:, None])[None, None]
    compressed_branch = by_heads(query_whole, summaries[None], allowed_comp, True)[0]
    nearby = jnp.concatenate([before, keys_values], axis=0).reshape(
        WINDOW + tok_count, GROUPS, 2 * HEAD_DIM
    )
    nearby = jnp.transpose(nearby, (1, 0, 2))[None]
    near_positions = first_pos - WINDOW + jnp.arange(WINDOW + tok_count, dtype=jnp.int32)
    allowed_win = (
        (near_positions[None, :] <= positions[:, None])
        & (near_positions[None, :] > positions[:, None] - WINDOW)
        & (near_positions[None, :] >= 0)
    )[None, None]
    window_branch = by_heads(query_whole, nearby, allowed_win, False)[0]
    gate_values = jax.nn.sigmoid(gate_logits.astype(jnp.float32)).reshape(
        3, tok_count, GROUPS, GROUP_HEADS, 1
    )
    attended = (
        gate_values[0] * compressed_branch
        + gate_values[1] * selected_branch
        + gate_values[2] * window_branch
    )
    return attended.reshape(tok_count, HEADS * HEAD_DIM).astype(jnp.bfloat16)


def solution(mesh):
    in_specs = (
        P(("grp", "seq"), None),
        P(("grp", "seq"), None),
        P(("grp", "seq"), None),
        P(None, ("grp", "seq"), None),
        P(),
        P(),
    )
    out_specs = P(("grp", "seq"), None)
    return jax.shard_map(shards, mesh=mesh, in_specs=in_specs, out_specs=out_specs, check_vma=False)
```

profile of v0, /device:TPU:0, one launch (start us, length us, event | category | flops | bytes accessed | tf_op | source)
XLA Modules:
  0.0 216.7 jit_solution(13625318544058351301)
XLA Ops:
  10.9 6.3 %all-to-all-start = ((s32[4,1,2]{2,1,0:T(1,128)}), s32[4,1,2]{2,1,0:T(1,128)}, u32[]{:S(2)}, u32[]{:S(2)}) async-start(s32[4,1,2]{2,1,0:T(1,128)} %copy.101), calls=%async_computation | async-start | bytes 4096 | tf_op jit(solution)/shard_map/all_to_all | solution.py:134
  18.9 2.6 %copy.97 = bf16[128,6144]{0,1:T(8,128)(2,1)} copy(bf16[128,6144]{1,0:T(8,128)(2,1)} %param.12) | data formatting | bytes 3145728 | tf_op args[0]
  22.0 42.4 %all_gather.6 = bf16[2,64,384]{2,0,1:T(2,128)(2,1)S(1)} all-gather(bf16[2,2,384]{2,0,1:T(2,128)(2,1)S(1)} %bitcast.261), channel_id=1, replica_groups=mesh['grp'=4,'seq'=8] {'grp','seq'}, dimensions={1}, use_global_device_ids=true | all-gather | bytes 101376 | tf_op jit(solution)/shard_map/all_gather | solution.py:123
  65.3 14.9 %while.33 = (s32[]{:T(128)}, f32[4,1,128,2,4,192]{2,5,4,0,3,1:T(8,128)S(1)}, s32[4]{0:T(128)}, bf16[1,128,2,16,192]{1,4,3,2,0:T(8,128)(2,1)}, bf16[1,2,64,384]{3...) while((s32[]{:T(128)}, ...), condition=%wide.region_4.5_spmd.clone, body=%wide.region_1.4_spmd.clone.sunk | while | flops 51128324 | bytes 2171823 | solution.py:66
  80.3 1.8 copy.106
  87.3 2.3 %gather_fusion.1 = bf16[8,64,384]{2,1,0:T(8,128)(2,1)} fusion(bf16[2,64,2,384]{3,1,2,0:T(8,128)(2,1)} %copy.106, s32[8]{0:T(128)S(1)} %reshape.547), kind=kCustom, calls=%fused_computation.1 | custom fusion | bytes 786496 | tf_op jit(solution)/shard_map/gather | solution.py:137
  89.6 3.5 %all-to-all-start.1 = ((bf16[4,2,64,384]{3,2,1,0:T(8,128)(2,1)}), bf16[4,2,64,384]{3,2,1,0:T(8,128)(2,1)S(1)}, u32[]{:S(2)}, u32[]{:S(2)}) async-start(bf16[4,2,64,384]{3,2,1,0:T(8,128)(2,1)} %bitcast.255), calls=%async_computation.1 | async-start | bytes 786432 | tf_op jit(solution)/shard_map/all_to_all | solution.py:136
  93.8 4.7 %reshape.537 = bf16[2,64,2,16,192]{4,3,2,1,0:T(8,128)(2,1)} reshape(bf16[128,6144]{1,0:T(8,128)(2,1)} %param.12) | data formatting | bytes 3145728 | tf_op jit(solution)/shard_map/reshape | solution.py:165
  99.1 6.4 %all-to-all-done.1 = bf16[4,2,64,384]{3,2,1,0:T(8,128)(2,1)S(1)} async-done(((bf16[4,2,64,384]{3,2,1,0:T(8,128)(2,1)}), bf16[4,2,64,384]{3,2,1,0:T(8,128)(2,1)S(1)}, u32[]{:S(2)}, u32[]{:S(2)}) %all-to-all-start.1) | async-done | bytes 393248 | tf_op jit(solution)/shard_map/all_to_all | solution.py:136
  105.5 2.7 %gather_fusion.2 = bf16[64,64,384]{2,1,0:T(8,128)(2,1)} fusion(bf16[4,2,64,384]{3,2,1,0:T(8,128)(2,1)S(1)} %all-to-all-done.1, s32[64]{0:T(128)S(1)} %reshape.553), kind=kCustom, calls=%fused_computation.2 | custom fusion | bytes 6291968 | tf_op jit(solution)/shard_map/gather | solution.py:145
  108.2 3.4 %reshape.538 = bf16[16,64,2,384]{3,2,1,0:T(2,128)(2,1)S(1)} reshape(bf16[1024,768]{1,0:T(8,128)(2,1)} %all-gather.2.cloned.1.call-done) | data formatting | bytes 3145728 | tf_op jit(solution)/shard_map/reshape | solution.py:148
  111.9 2.7 %gather_fusion = bf16[64,64,384]{2,1,0:T(8,128)(2,1)} fusion(bf16[16,64,2,384]{3,1,2,0:T(8,128)(2,1)S(1)} %copy.100, s32[64]{0:T(128)S(1)} %reshape.541), kind=kCustom, calls=%fused_computation | custom fusion | bytes 6291968 | tf_op jit(solution)/shard_map/gather | solution.py:149
  114.6 4.4 %broadcast_select_fusion = bf16[2,2,1024,384]{3,2,1,0:T(8,128)(2,1)} fusion(bf16[2,2,1024,384]{3,2,1,0:T(8,128)(2,1)} %bitcast.253, bf16[2,2,1024,384]{3,2,1,0:T(8,128)(2,1)} %bitcast.252, pred[2,2,1024]{2,1,0:T(4,128)(4,1)S(1)} %broadcast_in_dim.161), kind=kLoop, calls=%fused_computation.84 | loop fusion | flops 1572864 | bytes 9441280 | tf_op jit(solution)/shard_map/jit(_where)/select_n | solution.py:154
  119.0 3.2 %copy.108 = bf16[2,2,1024,384]{2,3,1,0:T(8,128)(2,1)S(1)} copy(bf16[2,2,1024,384]{3,2,1,0:T(8,128)(2,1)} %broadcast_select_fusion) | data formatting | bytes 6291456
  123.8 2.1 collective-permute-start
  125.9 30.6 %while.34 = (s32[]{:T(128)}, f32[4,2,64,2,4,192]{5,2,4,3,1,0:T(8,128)}, s32[4]{0:T(128)S(1)}, bf16[2,64,2,16,192]{4,3,2,1,0:T(8,128)(2,1)}, bf16[2,2,1024,384]{2...) while((s32[]{:T(128)}, ...), condition=%wide.region_12.13_spmd.clone, body=%wide.region_9.12_spmd.clone.sunk | while | flops 814416896 | bytes 18646196 | solution.py:66
  129.6 2.1 fusion.132
  137.3 2.1 fusion.132
  144.9 2.1 fusion.132
  147.0 1.8 fusion.133
  152.6 2.1 fusion.132
  156.4 11.7 %copy.121 = f32[2,64,2,4,4,192]{1,0,5,4,3,2:T(2,128)} copy(f32[2,64,2,4,4,192]{5,1,4,2,0,3:T(8,128)} %bitcast.16) | data formatting | bytes 6291456 | tf_op jit(solution)/shard_map/reshape;reshape | solution.py:166
  168.1 5.8 %reshape.575 = f32[128,6144]{0,1:T(8,128)S(1)} reshape(f32[2,64,2,4,4,192]{1,0,5,4,3,2:T(2,128)} %copy.121) | data formatting | bytes 6291456 | tf_op jit(solution)/shard_map/reshape;reshape | solution.py:166
  176.8 1.9 copy.111
  178.7 2.0 broadcast.656.clone2
  180.7 21.9 %while.35 = (s32[]{:T(128)}, f32[4,1,128,2,4,192]{2,5,4,0,3,1:T(8,128)}, s32[4]{0:T(128)S(1)}, bf16[1,128,2,16,192]{1,4,3,2,0:T(8,128)(2,1)}, bf16[1,2,256,384]{...) while((s32[]{:T(128)}, ...), condition=%wide.region_16.17_spmd.clone, body=%wide.region_13.16_spmd.clone.sunk | while | flops 204011520 | bytes 4873147 | solution.py:66
  184.0 2.2 %fusion.138 = f32[4,1,128,2,4,192]{2,5,4,0,3,1:T(8,128)} fusion(f32[4,1,128,2,4,192]{2,5,4,0,3,1:T(8,128)} %get-tuple-element.488, s32[]{:T(128)} %get-tuple-element.487, f32[1,2,4,128,256]{4,3,2,1,0:T(8,128)S(1)} %get-tuple-element.472, f32[2,4,128]{2,1,0:T(4,128)S(1)} %get-tuple-element.473, pred[128,256]{1,0:T(8,128)(4,1)S(1)} %and_and_fusion.2, ...), kind=kOutput, calls=%fused_computation.60.clone.1 | convolution fusion | flops 101646336 | bytes 2073088 | tf_op jit(solution)/shard_map/while/body/eval_jaxpr/bghtn,bgnd->bghtd/dot_general | solution.py:47
  189.4 2.2 %fusion.138 = f32[4,1,128,2,4,192]{2,5,4,0,3,1:T(8,128)} fusion(f32[4,1,128,2,4,192]{2,5,4,0,3,1:T(8,128)} %get-tuple-element.488, s32[]{:T(128)} %get-tuple-element.487, f32[1,2,4,128,256]{4,3,2,1,0:T(8,128)S(1)} %get-tuple-element.472, f32[2,4,128]{2,1,0:T(4,128)S(1)} %get-tuple-element.473, pred[128,256]{1,0:T(8,128)(4,1)S(1)} %and_and_fusion.2, ...), kind=kOutput, calls=%fused_computation.60.clone.1 | convolution fusion | flops 101646336 | bytes 2073088 | tf_op jit(solution)/shard_map/while/body/eval_jaxpr/bghtn,bgnd->bghtd/dot_general | solution.py:47
  194.9 2.2 %fusion.138 = f32[4,1,128,2,4,192]{2,5,4,0,3,1:T(8,128)} fusion(f32[4,1,128,2,4,192]{2,5,4,0,3,1:T(8,128)} %get-tuple-element.488, s32[]{:T(128)} %get-tuple-element.487, f32[1,2,4,128,256]{4,3,2,1,0:T(8,128)S(1)} %get-tuple-element.472, f32[2,4,128]{2,1,0:T(4,128)S(1)} %get-tuple-element.473, pred[128,256]{1,0:T(8,128)(4,1)S(1)} %and_and_fusion.2, ...), kind=kOutput, calls=%fused_computation.60.clone.1 | convolution fusion | flops 101646336 | bytes 2073088 | tf_op jit(solution)/shard_map/while/body/eval_jaxpr/bghtn,bgnd->bghtd/dot_general | solution.py:47
  200.4 2.3 %fusion.138 = f32[4,1,128,2,4,192]{2,5,4,0,3,1:T(8,128)} fusion(f32[4,1,128,2,4,192]{2,5,4,0,3,1:T(8,128)} %get-tuple-element.488, s32[]{:T(128)} %get-tuple-element.487, f32[1,2,4,128,256]{4,3,2,1,0:T(8,128)S(1)} %get-tuple-element.472, f32[2,4,128]{2,1,0:T(4,128)S(1)} %get-tuple-element.473, pred[128,256]{1,0:T(8,128)(4,1)S(1)} %and_and_fusion.2, ...), kind=kOutput, calls=%fused_computation.60.clone.1 | convolution fusion | flops 101646336 | bytes 2073088 | tf_op jit(solution)/shard_map/while/body/eval_jaxpr/bghtn,bgnd->bghtd/dot_general | solution.py:47
  202.6 4.6 %fusion.84 = bf16[128,6144]{0,1:T(8,128)(2,1)} fusion(f32[4,1,128,2,4,192]{2,5,4,0,3,1:T(8,128)} %get-tuple-element.103, f32[4,1,128,2,4,192]{2,5,4,0,3,1:T(8,128)} %copy-done.1, f32[128,6144]{0,1:T(8,128)S(1)} %reshape.575, f32[128,2,16]{0,2,1:T(8,128)S(1)} %bitcast.259, f32[128,2,16]{0,2,1:T(8,128)S(1)} %bitcast.260, f32[128,2,16]{0,2,1:T(8,128)S(1)} %bitcast.258), kind=kLoop, calls=%fused_computation.80 | loop fusion | flops 4718592 | bytes 11059200 | tf_op jit(solution)/shard_map/convert_element_type | solution.py:192
  207.3 2.6 %copy.113 = bf16[128,6144]{1,0:T(8,128)(2,1)} copy(bf16[128,6144]{0,1:T(8,128)(2,1)} %fusion.84) | data formatting | bytes 3145728 | tf_op jit(solution)/shard_map/convert_element_type | solution.py:192
  (155 shorter events, 58.9 us)
Async XLA Ops:
  6.5 15.3 %copy-start = (bf16[384,384]{1,0:T(8,128)(2,1)S(1)}, bf16[384,384]{1,0:T(8,128)(2,1)}, u32[]{:S(2)}) copy-start(bf16[384,384]{1,0:T(8,128)(2,1)} %param.17) | copy-start | bytes 884740
  6.5 15.0 %copy-start.3 = (bf16[64,384]{1,0:T(8,128)(2,1)S(1)}, bf16[64,384]{1,0:T(8,128)(2,1)}, u32[]{:S(2)}) copy-start(bf16[64,384]{1,0:T(8,128)(2,1)} %param.16) | copy-start | bytes 147460
  9.1 8.1 %copy-start.7 = (pred[2,32]{1,0:T(4,128)(4,1)}, pred[2,32]{1,0:T(4,128)(4,1)S(1)}, u32[]{:S(2)}) copy-start(pred[2,32]{1,0:T(4,128)(4,1)S(1)} %get-tuple-element.310) | copy-start | bytes 196
  9.1 8.1 %copy-start.8 = (pred[2,32]{1,0:T(4,128)(4,1)}, pred[2,32]{1,0:T(4,128)(4,1)S(1)}, u32[]{:S(2)}) copy-start(pred[2,32]{1,0:T(4,128)(4,1)S(1)} %get-tuple-element.293) | copy-start | bytes 196
  9.5 0.5 copy-start.5
  9.5 12.5 %copy-start.6 = (pred[64,4]{0,1:T(4,128)(4,1)}, pred[64,4]{0,1:T(4,128)(4,1)S(1)}, u32[]{:S(2)}) copy-start(pred[64,4]{0,1:T(4,128)(4,1)S(1)} %get-tuple-element.312) | copy-start | bytes 772
  10.9 75.5 %all-to-all-start = ((s32[4,1,2]{2,1,0:T(1,128)}), s32[4,1,2]{2,1,0:T(1,128)}, u32[]{:S(2)}, u32[]{:S(2)}) async-start(s32[4,1,2]{2,1,0:T(1,128)} %copy.101), calls=%async_computation | async-start | bytes 4096 | tf_op jit(solution)/shard_map/all_to_all | solution.py:134
  17.2 91.0 %all-gather.2.cloned.1.call-start = ((), (), s32[]{:S(2)}) async-start(), calls=%async_computation.2 | async-start | bytes 1769472 | tf_op jit(solution)/shard_map/all_gather | solution.py:146
  18.9 45.5 %copy-start.2 = (bf16[2,64,2,384]{3,2,1,0:T(2,128)(2,1)}, bf16[2,64,2,384]{3,2,1,0:T(2,128)(2,1)S(1)}, u32[]{:S(2)}) copy-start(bf16[2,64,2,384]{3,2,1,0:T(2,128)(2,1)S(1)} %reshape.535) | copy-start | bytes 589828
  80.2 9.4 %copy-start.1 = (f32[4,1,128,2,4,192]{2,5,4,0,3,1:T(8,128)}, f32[4,1,128,2,4,192]{2,5,4,0,3,1:T(8,128)S(1)}, u32[]{:S(2)}) copy-start(f32[4,1,128,2,4,192]{2,5,4,0,3,1:T(8,128)S(1)} %get-tuple-element.101) | copy-start | bytes 9437188
  80.2 18.9 %copy-start.4 = (bf16[3,128,32]{1,2,0:T(8,128)(2,1)S(1)}, bf16[3,128,32]{1,2,0:T(8,128)(2,1)}, u32[]{:S(2)}) copy-start(bf16[3,128,32]{1,2,0:T(8,128)(2,1)} %param.15) | copy-start | bytes 73732
  89.6 15.9 %all-to-all-start.1 = ((bf16[4,2,64,384]{3,2,1,0:T(8,128)(2,1)}), bf16[4,2,64,384]{3,2,1,0:T(8,128)(2,1)S(1)}, u32[]{:S(2)}, u32[]{:S(2)}) async-start(bf16[4,2,64,384]{3,2,1,0:T(8,128)(2,1)} %bitcast.255), calls=%async_computation.1 | async-start | bytes 786432 | tf_op jit(solution)/shard_map/all_to_all | solution.py:136
  123.8 50.2 %collective-permute-start = (bf16[128,768]{1,0:T(8,128)(2,1)}, bf16[128,768]{1,0:T(8,128)(2,1)}, u32[]{:S(2)}, u32[]{:S(2)}) collective-permute-start(bf16[128,768]{1,0:T(8,128)(2,1)} %slice.52), channel_id=1, source_target_pairs={{0,8},{8,16},{16,24},{1,9},{9,17},{17,25},{2,10},{10,18},{18,26},{... | collective-permute-start | bytes 589832 | tf_op jit(solution)/shard_map/ppermute | solution.py:21
Sparse Core Ops, SparseCore 0:
  19.9 27.4 all-gather.1
where the time goes:
time: 218 us; the launch traced here: 217 us
  local copies, waits for them, and re-layouts  74.2 us (34%)
  blocking collectives  42.4 us (19%)
  matrix products  31.7 us (15%)
  other arithmetic  28.2 us (13%)
  between operations  13.7 us (6%)
  starting transfers between devices  11.9 us (5%)
  loops' own time  7.63 us (4%)
  waiting for transfers between devices  7.09 us (3%)
    all_gather x1, blocking collectives, shards(): lax.all_gather(local_summary, ('grp', 'seq'), axis=1, tiled=True)  42.4 us
    dot_general x12, matrix products, attend(): jnp.einsum('bghtn,bgnd->bghtd', rounded, key_block[..., head_dim:], prefe...  17.7 us
    another operation x2, local copies, waits for them, and re-layouts, shards(): by_heads(query_blocks, chosen, allowed_sel, False)  17.5 us
    dot_general x12, matrix products, attend(): jnp.einsum('btghd,bgnd->bghtn', query_block, key_block[..., :head_dim], p...  13.8 us
    dynamic_slice x12, local copies, waits for them, and re-layouts, by_heads(): lax.map(head_slab, jnp.arange(head_count // slab_width, dtype=jnp.int32))  9.99 us
    sub x4, other arithmetic, attend(): weights = jnp.where(allowed_wide, jnp.exp(scores - top_score), 0.0)  8.59 us
    another operation x3, loops' own time, by_heads(): lax.map(head_slab, jnp.arange(head_count // slab_width, dtype=jnp.int32))  7.63 us
    all_to_all x1, waiting for transfers between devices, shards(): lax.all_to_all(local_view[asked_clipped % dev_blocks, :, asked_clipped //...  6.38 us
  transfers between devices with their start and end apart: 4, of which 1 were waited for; matrix products, arithmetic and copies ran while one was open for 37% of the time, Pallas kernels for 0%

commit v1 on v0

--- a/solution.py
+++ b/solution.py
@@ -13,6 +13,18 @@
 CAP = 2
 WINDOW = 128
 NEG_FILL = -1e30
+
+
+def collect(x, axis, dim):
+    ways, here, lap = (lax.axis_size(axis), lax.axis_index(axis), x.shape[dim])
+    line, have = (x, 1)
+    while have < ways:
+        line = jnp.concatenate(
+            [line, lax.ppermute(line, axis, [(d, (d - have) % ways) for d in range(ways)])],
+            axis=dim,
+        )
+        have = 2 * have
+    return jnp.roll(line, here * lap, axis=dim)
 
 
 def from_behind(block, axis, distance):
@@ -120,7 +132,7 @@
     local_summary = jnp.transpose(
         compress_blocks(keys_values, pos_weight, compress_weight), (1, 0, 2)
     )
-    summaries = lax.all_gather(local_summary, ("grp", "seq"), axis=1, tiled=True)
+    summaries = collect(local_summary, ("grp", "seq"), 1)
     picked = selection.reshape(dev_blocks, GROUPS, TOP)
     group_ids = jnp.broadcast_to(jnp.arange(GROUPS, dtype=jnp.int32)[None, :, None], picked.shape)
     flat_groups = group_ids.reshape(-1)

time: 218 us -> 182 us (0.83)
  the two profiles are of different devices: /device:TPU:0 before, /device:TPU:6 now
where the time goes in v1:
time: 182 us; the launch traced here: 180 us
  local copies, waits for them, and re-layouts  63.9 us (35%)
  matrix products  31.2 us (17%)
  other arithmetic  28.1 us (15%)
  starting transfers between devices  26.1 us (14%)
  between operations  13.7 us (8%)
  waiting for transfers between devices  9.57 us (5%)
  loops' own time  7.43 us (4%)
    dot_general x12, matrix products, attend(): jnp.einsum('bghtn,bgnd->bghtd', rounded, key_block[..., head_dim:], prefe...  21.3 us
    another operation x2, local copies, waits for them, and re-layouts, shards(): by_heads(query_blocks, chosen, allowed_sel, False)  17.5 us
    ppermute x5, starting transfers between devices, collect(): lax.ppermute(line, axis, [(d, (d - have) % ways) for d in range(ways)])  11.4 us
    dot_general x12, matrix products, attend(): jnp.einsum('btghd,bgnd->bghtn', query_block, key_block[..., :head_dim], p...  9.82 us
    ppermute x5, waiting for transfers between devices, collect(): lax.ppermute(line, axis, [(d, (d - have) % ways) for d in range(ways)])  8.85 us
    sub x4, other arithmetic, attend(): weights = jnp.where(allowed_wide, jnp.exp(scores - top_score), 0.0)  8.59 us
    another operation x3, loops' own time, by_heads(): lax.map(head_slab, jnp.arange(head_count // slab_width, dtype=jnp.int32))  7.43 us
    dynamic_slice x12, local copies, waits for them, and re-layouts, by_heads(): lax.map(head_slab, jnp.arange(head_count // slab_width, dtype=jnp.int32))  6.96 us
  transfers between devices with their start and end apart: 9, of which 3 were waited for; matrix products, arithmetic and copies ran while one was open for 39% of the time, Pallas kernels for 0%

profile of v1, /device:TPU:6, one launch (start us, length us, event | category | flops | bytes accessed | tf_op | source)
XLA Modules:
  0.0 180.0 jit_solution(8192941719297254235)
XLA Ops:
  9.7 4.9 %all-to-all-start = ((s32[4,1,2]{2,1,0:T(1,128)}), s32[4,1,2]{2,1,0:T(1,128)S(1)}, u32[]{:S(2)}, u32[]{:S(2)}) async-start(s32[4,1,2]{2,1,0:T(1,128)} %copy.101), calls=%async_computation | async-start | bytes 4096 | tf_op jit(solution)/shard_map/all_to_all | solution.py:146
  19.5 3.4 %reshape.537 = bf16[2,64,2,16,192]{4,3,2,1,0:T(8,128)(2,1)} reshape(bf16[128,6144]{1,0:T(8,128)(2,1)S(1)} %copy-done.2) | data formatting | bytes 3145728 | tf_op jit(solution)/shard_map/reshape | solution.py:177
  22.9 1.9 %copy.97 = bf16[128,6144]{0,1:T(8,128)(2,1)S(1)} copy(bf16[128,6144]{1,0:T(8,128)(2,1)} %param.12) | data formatting | bytes 3145728 | tf_op args[0]
  26.7 4.3 %collective-permute-done.1 = bf16[2,4,384]{2,0,1:T(2,128)(2,1)S(1)} collective-permute-done((bf16[2,4,384]{2,0,1:T(2,128)(2,1)S(1)}, bf16[2,4,384]{2,0,1:T(2,128)(2,1)S(1)}, u32[]{:S(2)}, u32[]{:S(2)}) %collective-permute-start.1) | collective-permute-done | bytes 6176 | tf_op jit(solution)/shard_map/ppermute | solution.py:23
  32.6 3.0 %collective-permute-done.2 = bf16[2,8,384]{2,0,1:T(2,128)(2,1)S(1)} collective-permute-done((bf16[2,8,384]{2,0,1:T(2,128)(2,1)S(1)}, bf16[2,8,384]{2,0,1:T(2,128)(2,1)S(1)}, u32[]{:S(2)}, u32[]{:S(2)}) %collective-permute-start.2) | collective-permute-done | bytes 12320 | tf_op jit(solution)/shard_map/ppermute | solution.py:23
  35.7 7.7 %collective-permute-start.3 = (bf16[2,16,384]{2,0,1:T(2,128)(2,1)S(1)}, bf16[2,16,384]{2,0,1:T(2,128)(2,1)S(1)}, u32[]{:S(2)}, u32[]{:S(2)}) collective-permute-start(bf16[2,16,384]{2,0,1:T(2,128)(2,1)S(1)} %pad_maximum_fusion.1), channel_id=1, source_target_pairs={{0,24},{1,25},{2,26},{3,27},{4,28},{5,29},{6,30},{7,31},{8,0},{9,1... | collective-permute-start | bytes 73736 | tf_op jit(solution)/shard_map/ppermute | solution.py:23
  47.4 5.1 %all-to-all-start.1 = ((bf16[4,2,64,384]{3,2,1,0:T(8,128)(2,1)}), bf16[4,2,64,384]{3,2,1,0:T(8,128)(2,1)S(1)}, u32[]{:S(2)}, u32[]{:S(2)}) async-start(bf16[4,2,64,384]{3,2,1,0:T(8,128)(2,1)} %bitcast.14), calls=%async_computation.1 | async-start | bytes 786432 | tf_op jit(solution)/shard_map/all_to_all | solution.py:148
  52.8 2.1 %broadcast.657.clone2.1 = f32[4,1,128,2,4,192]{2,5,4,0,3,1:T(8,128)} broadcast(f32[]{:T(128)} %constant.203.clone.1), dimensions={} | broadcast | bytes 3145732 | tf_op jit(solution)/shard_map/broadcast.30
  55.0 11.8 %while.33 = (s32[]{:T(128)}, f32[4,1,128,2,4,192]{2,5,4,0,3,1:T(8,128)}, s32[4]{0:T(128)S(1)}, bf16[1,128,2,16,192]{1,4,3,2,0:T(8,128)(2,1)S(1)}, bf16[1,2,64,38...) while((s32[]{:T(128)}, ...), condition=%wide.region_4.5_spmd.clone, body=%wide.region_1.4_spmd.clone.sunk | while | flops 51128324 | bytes 2172331 | solution.py:78
  66.8 2.7 %gather_fusion.2 = bf16[64,64,384]{2,1,0:T(8,128)(2,1)} fusion(bf16[4,2,64,384]{3,2,1,0:T(8,128)(2,1)S(1)} %all-to-all-done.1, s32[64]{0:T(128)S(1)} %reshape.553), kind=kCustom, calls=%fused_computation.2 | custom fusion | bytes 6291968 | tf_op jit(solution)/shard_map/gather | solution.py:157
  69.5 3.4 %reshape.538 = bf16[16,64,2,384]{3,2,1,0:T(2,128)(2,1)S(1)} reshape(bf16[1024,768]{1,0:T(8,128)(2,1)} %all-gather.2.cloned.1.call-done) | data formatting | bytes 3145728 | tf_op jit(solution)/shard_map/reshape | solution.py:160
  73.2 2.7 %gather_fusion = bf16[64,64,384]{2,1,0:T(8,128)(2,1)} fusion(bf16[16,64,2,384]{3,1,2,0:T(8,128)(2,1)S(1)} %copy.100, s32[64]{0:T(128)S(1)} %reshape.541), kind=kCustom, calls=%fused_computation | custom fusion | bytes 6291968 | tf_op jit(solution)/shard_map/gather | solution.py:161
  75.9 4.4 %broadcast_select_fusion = bf16[2,2,1024,384]{3,2,1,0:T(8,128)(2,1)} fusion(bf16[2,2,1024,384]{3,2,1,0:T(8,128)(2,1)} %bitcast.258, bf16[2,2,1024,384]{3,2,1,0:T(8,128)(2,1)} %bitcast.257, pred[2,2,1024]{2,1,0:T(4,128)(4,1)S(1)} %broadcast_in_dim.161), kind=kLoop, calls=%fused_computation.84 | loop fusion | flops 1572864 | bytes 9441280 | tf_op jit(solution)/shard_map/jit(_where)/select_n | solution.py:166
  80.2 3.2 %copy.108 = bf16[2,2,1024,384]{2,3,1,0:T(8,128)(2,1)S(1)} copy(bf16[2,2,1024,384]{3,2,1,0:T(8,128)(2,1)} %broadcast_select_fusion) | data formatting | bytes 6291456
  85.0 4.8 %collective-permute-start.5 = (bf16[128,768]{1,0:T(8,128)(2,1)}, bf16[128,768]{1,0:T(8,128)(2,1)}, u32[]{:S(2)}, u32[]{:S(2)}) collective-permute-start(bf16[128,768]{1,0:T(8,128)(2,1)} %slice.52), channel_id=1, source_target_pairs={{0,8},{8,16},{16,24},{1,9},{9,17},{17,25},{2,10},{10,18},{18,26},{... | collective-permute-start | bytes 589832 | tf_op jit(solution)/shard_map/ppermute | solution.py:33
  89.8 30.0 %while.34 = (s32[]{:T(128)}, f32[4,2,64,2,4,192]{5,2,4,3,1,0:T(8,128)}, s32[4]{0:T(128)S(1)}, bf16[2,64,2,16,192]{4,3,2,1,0:T(8,128)(2,1)}, bf16[2,2,1024,384]{2...) while((s32[]{:T(128)}, ...), condition=%wide.region_12.13_spmd.clone, body=%wide.region_9.12_spmd.clone.sunk | while | flops 814416896 | bytes 18646196 | solution.py:78
  93.4 2.1 %fusion.132 = (f32[2,2,4,64]{3,2,1,0:T(4,128)S(1)}, bf16[2,2,4,64,1024]{4,3,2,1,0:T(8,128)(2,1)S(1)}) fusion(f32[2,2,64,4,1024]{4,2,3,1,0:T(8,128)S(1)} %fusion.131, pred[2,2,64,1024]{3,2,1,0:T(8,128)(4,1)S(1)} %compare_and_fusion.4), kind=kOutput, calls=%fused_computation.166.clone.1 | output fusion | flops 8389631 | bytes 6557696 | tf_op jit(solution)/shard_map/while/body/eval_jaxpr/sub | solution.py:53
  101.0 2.1 %fusion.132 = (f32[2,2,4,64]{3,2,1,0:T(4,128)S(1)}, bf16[2,2,4,64,1024]{4,3,2,1,0:T(8,128)(2,1)S(1)}) fusion(f32[2,2,64,4,1024]{4,2,3,1,0:T(8,128)S(1)} %fusion.131, pred[2,2,64,1024]{3,2,1,0:T(8,128)(4,1)S(1)} %compare_and_fusion.4), kind=kOutput, calls=%fused_computation.166.clone.1 | output fusion | flops 8389631 | bytes 6557696 | tf_op jit(solution)/shard_map/while/body/eval_jaxpr/sub | solution.py:53
  108.5 2.1 %fusion.132 = (f32[2,2,4,64]{3,2,1,0:T(4,128)S(1)}, bf16[2,2,4,64,1024]{4,3,2,1,0:T(8,128)(2,1)S(1)}) fusion(f32[2,2,64,4,1024]{4,2,3,1,0:T(8,128)S(1)} %fusion.131, pred[2,2,64,1024]{3,2,1,0:T(8,128)(4,1)S(1)} %compare_and_fusion.4), kind=kOutput, calls=%fused_computation.166.clone.1 | output fusion | flops 8389631 | bytes 6557696 | tf_op jit(solution)/shard_map/while/body/eval_jaxpr/sub | solution.py:53
  110.6 1.8 fusion.133
  116.0 2.1 %fusion.132 = (f32[2,2,4,64]{3,2,1,0:T(4,128)S(1)}, bf16[2,2,4,64,1024]{4,3,2,1,0:T(8,128)(2,1)S(1)}) fusion(f32[2,2,64,4,1024]{4,2,3,1,0:T(8,128)S(1)} %fusion.131, pred[2,2,64,1024]{3,2,1,0:T(8,128)(4,1)S(1)} %compare_and_fusion.4), kind=kOutput, calls=%fused_computation.166.clone.1 | output fusion | flops 8389631 | bytes 6557696 | tf_op jit(solution)/shard_map/while/body/eval_jaxpr/sub | solution.py:53
  119.9 11.7 %copy.121 = f32[2,64,2,4,4,192]{1,0,5,4,3,2:T(2,128)} copy(f32[2,64,2,4,4,192]{5,1,4,2,0,3:T(8,128)} %bitcast.16) | data formatting | bytes 6291456 | tf_op jit(solution)/shard_map/reshape;reshape | solution.py:178
  131.6 5.8 %reshape.575 = f32[128,6144]{0,1:T(8,128)S(1)} reshape(f32[2,64,2,4,4,192]{1,0,5,4,3,2:T(2,128)} %copy.121) | data formatting | bytes 6291456 | tf_op jit(solution)/shard_map/reshape;reshape | solution.py:178
  140.2 1.9 %copy.111 = bf16[256,768]{0,1:T(8,128)(2,1)} copy(bf16[256,768]{1,0:T(8,128)(2,1)} %pad_maximum_fusion) | data formatting | bytes 786432 | tf_op jit(solution)/shard_map/concatenate | solution.py:185
  142.1 2.0 %broadcast.657.clone2 = f32[4,1,128,2,4,192]{2,5,4,0,3,1:T(8,128)} broadcast(f32[]{:T(128)} %constant.203.clone.1), dimensions={} | broadcast | bytes 3145732 | tf_op jit(solution)/shard_map/broadcast.30
  144.1 21.9 %while.35 = (s32[]{:T(128)}, f32[4,1,128,2,4,192]{2,5,4,0,3,1:T(8,128)}, s32[4]{0:T(128)S(1)}, bf16[1,128,2,16,192]{1,4,3,2,0:T(8,128)(2,1)}, bf16[1,2,256,384]{...) while((s32[]{:T(128)}, ...), condition=%wide.region_16.17_spmd.clone, body=%wide.region_13.16_spmd.clone.sunk | while | flops 204011520 | bytes 4873147 | solution.py:78
  147.3 2.2 %fusion.138 = f32[4,1,128,2,4,192]{2,5,4,0,3,1:T(8,128)} fusion(f32[4,1,128,2,4,192]{2,5,4,0,3,1:T(8,128)} %get-tuple-element.472, s32[]{:T(128)} %get-tuple-element.471, f32[1,2,4,128,256]{4,3,2,1,0:T(8,128)S(1)} %get-tuple-element.456, f32[2,4,128]{2,1,0:T(4,128)S(1)} %get-tuple-element.457, pred[128,256]{1,0:T(8,128)(4,1)S(1)} %and_and_fusion.2, ...), kind=kOutput, calls=%fused_computation.60.clone.1 | convolution fusion | flops 101646336 | bytes 2073088 | tf_op jit(solution)/shard_map/while/body/eval_jaxpr/bghtn,bgnd->bghtd/dot_general | solution.py:59
  152.8 2.3 %fusion.138 = f32[4,1,128,2,4,192]{2,5,4,0,3,1:T(8,128)} fusion(f32[4,1,128,2,4,192]{2,5,4,0,3,1:T(8,128)} %get-tuple-element.472, s32[]{:T(128)} %get-tuple-element.471, f32[1,2,4,128,256]{4,3,2,1,0:T(8,128)S(1)} %get-tuple-element.456, f32[2,4,128]{2,1,0:T(4,128)S(1)} %get-tuple-element.457, pred[128,256]{1,0:T(8,128)(4,1)S(1)} %and_and_fusion.2, ...), kind=kOutput, calls=%fused_computation.60.clone.1 | convolution fusion | flops 101646336 | bytes 2073088 | tf_op jit(solution)/shard_map/while/body/eval_jaxpr/bghtn,bgnd->bghtd/dot_general | solution.py:59
  158.2 2.2 %fusion.138 = f32[4,1,128,2,4,192]{2,5,4,0,3,1:T(8,128)} fusion(f32[4,1,128,2,4,192]{2,5,4,0,3,1:T(8,128)} %get-tuple-element.472, s32[]{:T(128)} %get-tuple-element.471, f32[1,2,4,128,256]{4,3,2,1,0:T(8,128)S(1)} %get-tuple-element.456, f32[2,4,128]{2,1,0:T(4,128)S(1)} %get-tuple-element.457, pred[128,256]{1,0:T(8,128)(4,1)S(1)} %and_and_fusion.2, ...), kind=kOutput, calls=%fused_computation.60.clone.1 | convolution fusion | flops 101646336 | bytes 2073088 | tf_op jit(solution)/shard_map/while/body/eval_jaxpr/bghtn,bgnd->bghtd/dot_general | solution.py:59
  163.7 2.3 %fusion.138 = f32[4,1,128,2,4,192]{2,5,4,0,3,1:T(8,128)} fusion(f32[4,1,128,2,4,192]{2,5,4,0,3,1:T(8,128)} %get-tuple-element.472, s32[]{:T(128)} %get-tuple-element.471, f32[1,2,4,128,256]{4,3,2,1,0:T(8,128)S(1)} %get-tuple-element.456, f32[2,4,128]{2,1,0:T(4,128)S(1)} %get-tuple-element.457, pred[128,256]{1,0:T(8,128)(4,1)S(1)} %and_and_fusion.2, ...), kind=kOutput, calls=%fused_computation.60.clone.1 | convolution fusion | flops 101646336 | bytes 2073088 | tf_op jit(solution)/shard_map/while/body/eval_jaxpr/bghtn,bgnd->bghtd/dot_general | solution.py:59
  166.0 4.6 %fusion.84 = bf16[128,6144]{0,1:T(8,128)(2,1)} fusion(f32[4,1,128,2,4,192]{2,5,4,0,3,1:T(8,128)} %get-tuple-element.103, f32[4,1,128,2,4,192]{2,5,4,0,3,1:T(8,128)} %get-tuple-element.101, f32[128,6144]{0,1:T(8,128)S(1)} %reshape.575, f32[128,2,16]{0,2,1:T(8,128)S(1)} %bitcast.267, f32[128,2,16]{0,2,1:T(8,128)S(1)} %bitcast.268, f32[128,2,16]{0,2,1:T(8,128)S(1)} %bitcast.266), kind=kLoop, calls=%fused_computation.80 | loop fusion | flops 4718592 | bytes 11059200 | tf_op jit(solution)/shard_map/convert_element_type | solution.py:204
  170.6 2.6 %copy.113 = bf16[128,6144]{1,0:T(8,128)(2,1)} copy(bf16[128,6144]{0,1:T(8,128)(2,1)} %fusion.84) | data formatting | bytes 3145728 | tf_op jit(solution)/shard_map/convert_element_type | solution.py:204
  (167 shorter events, 57.3 us)
Async XLA Ops:
  6.5 10.8 %copy-start = (bf16[384,384]{1,0:T(8,128)(2,1)S(1)}, bf16[384,384]{1,0:T(8,128)(2,1)}, u32[]{:S(2)}) copy-start(bf16[384,384]{1,0:T(8,128)(2,1)} %param.17) | copy-start | bytes 884740
  6.5 13.0 %copy-start.2 = (bf16[128,6144]{1,0:T(8,128)(2,1)S(1)}, bf16[128,6144]{1,0:T(8,128)(2,1)}, u32[]{:S(2)}) copy-start(bf16[128,6144]{1,0:T(8,128)(2,1)} %param.12) | copy-start | bytes 4718596
  9.7 15.7 %all-to-all-start = ((s32[4,1,2]{2,1,0:T(1,128)}), s32[4,1,2]{2,1,0:T(1,128)S(1)}, u32[]{:S(2)}, u32[]{:S(2)}) async-start(s32[4,1,2]{2,1,0:T(1,128)} %copy.101), calls=%async_computation | async-start | bytes 4096 | tf_op jit(solution)/shard_map/all_to_all | solution.py:146
  14.6 54.9 %all-gather.2.cloned.1.call-start = ((), (), s32[]{:S(2)}) async-start(), calls=%async_computation.2 | async-start | bytes 1769472 | tf_op jit(solution)/shard_map/all_gather | solution.py:158
  17.5 8.0 %collective-permute-start = (bf16[2,2,384]{2,0,1:T(2,128)(2,1)S(1)}, bf16[2,2,384]{2,0,1:T(2,128)(2,1)S(1)}, u32[]{:S(2)}, u32[]{:S(2)}) collective-permute-start(bf16[2,2,384]{2,0,1:T(2,128)(2,1)S(1)} %bitcast.262), channel_id=1, source_target_pairs={{0,31},{1,0},{2,1},{3,2},{4,3},{5,4},{6,5},{7,6},{8,7},{9,8},{10,9... | collective-permute-start | bytes 9224 | tf_op jit(solution)/shard_map/ppermute | solution.py:23
  25.5 5.5 %collective-permute-start.1 = (bf16[2,4,384]{2,0,1:T(2,128)(2,1)S(1)}, bf16[2,4,384]{2,0,1:T(2,128)(2,1)S(1)}, u32[]{:S(2)}, u32[]{:S(2)}) collective-permute-start(bf16[2,4,384]{2,0,1:T(2,128)(2,1)S(1)} %pad_maximum_fusion.3), channel_id=1, source_target_pairs={{0,30},{1,31},{2,0},{3,1},{4,2},{5,3},{6,4},{7,5},{8,6},{9,7},{10,... | collective-permute-start | bytes 18440 | tf_op jit(solution)/shard_map/ppermute | solution.py:23
  31.0 4.6 %collective-permute-start.2 = (bf16[2,8,384]{2,0,1:T(2,128)(2,1)S(1)}, bf16[2,8,384]{2,0,1:T(2,128)(2,1)S(1)}, u32[]{:S(2)}, u32[]{:S(2)}) collective-permute-start(bf16[2,8,384]{2,0,1:T(2,128)(2,1)S(1)} %pad_maximum_fusion.2), channel_id=1, source_target_pairs={{0,28},{1,29},{2,30},{3,31},{4,0},{5,1},{6,2},{7,3},{8,4},{9,5},{1... | collective-permute-start | bytes 36872 | tf_op jit(solution)/shard_map/ppermute | solution.py:23
  35.7 9.2 %collective-permute-start.3 = (bf16[2,16,384]{2,0,1:T(2,128)(2,1)S(1)}, bf16[2,16,384]{2,0,1:T(2,128)(2,1)S(1)}, u32[]{:S(2)}, u32[]{:S(2)}) collective-permute-start(bf16[2,16,384]{2,0,1:T(2,128)(2,1)S(1)} %pad_maximum_fusion.1), channel_id=1, source_target_pairs={{0,24},{1,25},{2,26},{3,27},{4,28},{5,29},{6,30},{7,31},{8,0},{9,1... | collective-permute-start | bytes 73736 | tf_op jit(solution)/shard_map/ppermute | solution.py:23
  45.0 7.6 %collective-permute-start.4 = (bf16[2,32,384]{2,0,1:T(2,128)(2,1)S(1)}, bf16[2,32,384]{2,0,1:T(2,128)(2,1)S(1)}, u32[]{:S(2)}, u32[]{:S(2)}) collective-permute-start(bf16[2,32,384]{2,0,1:T(2,128)(2,1)S(1)} %get-tuple-element.276), channel_id=1, source_target_pairs={{0,16},{1,17},{2,18},{3,19},{4,20},{5,21},{6,22},{7,23},{8,24},{9,... | collective-permute-start | bytes 147464 | tf_op jit(solution)/shard_map/ppermute | solution.py:23
  47.4 19.4 %all-to-all-start.1 = ((bf16[4,2,64,384]{3,2,1,0:T(8,128)(2,1)}), bf16[4,2,64,384]{3,2,1,0:T(8,128)(2,1)S(1)}, u32[]{:S(2)}, u32[]{:S(2)}) async-start(bf16[4,2,64,384]{3,2,1,0:T(8,128)(2,1)} %bitcast.14), calls=%async_computation.1 | async-start | bytes 786432 | tf_op jit(solution)/shard_map/all_to_all | solution.py:148
  66.8 2.7 %copy-start.1 = (bf16[1,128,2,16,192]{1,4,3,2,0:T(8,128)(2,1)}, bf16[1,128,2,16,192]{1,4,3,2,0:T(8,128)(2,1)S(1)}, u32[]{:S(2)}) copy-start(bf16[1,128,2,16,192]{1,4,3,2,0:T(8,128)(2,1)S(1)} %get-tuple-element.568) | copy-start | bytes 4718596
  85.0 52.4 %collective-permute-start.5 = (bf16[128,768]{1,0:T(8,128)(2,1)}, bf16[128,768]{1,0:T(8,128)(2,1)}, u32[]{:S(2)}, u32[]{:S(2)}) collective-permute-start(bf16[128,768]{1,0:T(8,128)(2,1)} %slice.52), channel_id=1, source_target_pairs={{0,8},{8,16},{16,24},{1,9},{9,17},{17,25},{2,10},{10,18},{18,26},{... | collective-permute-start | bytes 589832 | tf_op jit(solution)/shard_map/ppermute | solution.py:33
Sparse Core Ops, SparseCore 0:
  17.3 26.2 all-gather.1
